TPU v7x, 512 devices: a whole 4x8x8 slice. The times are simulated.
512 devices in a mesh: pair: 32 (over y_lo, z), day: 16 (over y_hi, x, core).
Axes of the slice: x: 4, y: 8 (y_hi: 2, y_lo: 4; y = y_hi * 4 + y_lo), z: 8, core: 2. Of those that a mesh axis runs over, the one named last changes fastest.
Arguments:
- spectra: bfloat16 [32, 2, 2048, 1024], P('day', None, 'pair'), may hold values from -6 to 6
- band_weights: float32 [8, 2048], replicated, may hold values from 0.05 to 1
- pair_stations: int32 [1536, 2], replicated, may hold values from 0 to 1023
- block_live: int32 [512], P(('pair', 'day')), may hold values from 1 to 3, 1152 in all
- windows: int32 [1536, 8, 2], P(('pair', 'day')), may hold values from 0 to 4096, as said below
- observed: bfloat16 [1536, 8, 4096], P(('pair', 'day')), may hold values from -6 to 6
Outputs:
- adjoint: float32 [32, 2, 2048, 1024], P('day', None, 'pair')
Inputs may be any that keep to these rules, and one draw needn't show every extreme that they name: Block b holds pairs b * 3 to b * 3 + 2, and its first block_live[b] pairs are live. windows[p, k, 0] < windows[p, k, 1].
All inputs are finite; a program needn't handle non-finite values.
Results may differ from a plain program's by a relative error of at most 0.0035.
Values sent between devices are 32-bit elements; how exact they have to be, the bound alone decides.
A program may use at most 64 MiB of HBM per device.

v0:
```python
import math
import jax
import jax.numpy as jnp
from jax import lax
from jax.sharding import PartitionSpec as P


def table_block(start, width, lags):
    half = lags // 2
    freqs = jnp.arange(half, dtype=jnp.int32)
    lag_index = start + jnp.arange(width, dtype=jnp.int32)
    phase = freqs[:, None] * lag_index[None, :] % lags
    angle = phase.astype(jnp.float32) * (2.0 * math.pi / lags)
    return jnp.concatenate([jnp.cos(angle), -jnp.sin(angle)], axis=0).astype(jnp.bfloat16)


def one_hot_rows(identity, columns):
    return (identity[:, None] == columns[None, :]).astype(jnp.bfloat16)


def gather_rows(flat_spectra, stations):
    count = stations.shape[0]
    station_count = flat_spectra.shape[1]
    width = math.gcd(count, 512)
    columns = jnp.arange(station_count, dtype=jnp.int32)
    dims = (((1,), (1,)), ((), ()))

    def gather_step(index, buffers):
        start = index * width
        identity = lax.dynamic_slice_in_dim(stations, start, width, 0)
        first_hot = one_hot_rows(identity[:, 0], columns)
        second_hot = one_hot_rows(identity[:, 1], columns)
        first_part = lax.dot_general(
            flat_spectra, first_hot, dims, preferred_element_type=jnp.float32
        ).astype(jnp.bfloat16)
        second_part = lax.dot_general(
            flat_spectra, second_hot, dims, preferred_element_type=jnp.float32
        ).astype(jnp.bfloat16)
        return (
            lax.dynamic_update_slice_in_dim(buffers[0], first_part, start, 1),
            lax.dynamic_update_slice_in_dim(buffers[1], second_part, start, 1),
        )

    empty = jnp.zeros((flat_spectra.shape[0], count), jnp.bfloat16)
    return lax.fori_loop(0, count // width, gather_step, (empty, empty))


def cross_stack(first_rows, second_rows, day_count, freq_count):
    count = first_rows.shape[1]
    first = first_rows.reshape(day_count, 2, freq_count, count).astype(jnp.float32)
    second = second_rows.reshape(day_count, 2, freq_count, count).astype(jnp.float32)
    real_part = jnp.sum(first[:, 0] * second[:, 0] + first[:, 1] * second[:, 1], axis=0)
    imag_part = jnp.sum(first[:, 0] * second[:, 1] - first[:, 1] * second[:, 0], axis=0)
    return jnp.stack([real_part, imag_part]).transpose(0, 2, 1)


def add_to_stations(accum, to_first, to_second, stations):
    count = stations.shape[0]
    station_count = accum.shape[1]
    width = math.gcd(count, 512)
    columns = jnp.arange(station_count, dtype=jnp.int32)

    def add_step(index, total):
        start = index * width
        identity = lax.dynamic_slice_in_dim(stations, start, width, 0)
        hot = jnp.concatenate(
            [one_hot_rows(identity[:, 0], columns), one_hot_rows(identity[:, 1], columns)], axis=0
        )
        terms = jnp.concatenate(
            [
                lax.dynamic_slice_in_dim(to_first, start, width, 1),
                lax.dynamic_slice_in_dim(to_second, start, width, 1),
            ],
            axis=1,
        )
        return total + jnp.dot(
            terms,
            hot.astype(jnp.float32),
            precision=lax.Precision.HIGHEST,
            preferred_element_type=jnp.float32,
        )

    return lax.fori_loop(0, count // width, add_step, accum)


def station_terms(accum, first_rows, second_rows, grads, stations, day_count):
    count = first_rows.shape[1]
    freq_count = grads.shape[2]
    first = first_rows.reshape(day_count, 2, freq_count, count).astype(jnp.float32)
    second = second_rows.reshape(day_count, 2, freq_count, count).astype(jnp.float32)
    turned = grads.transpose(0, 2, 1)
    grad_real = turned[0][None]
    grad_imag = turned[1][None]
    to_first = jnp.stack(
        [
            grad_real * second[:, 0] + grad_imag * second[:, 1],
            grad_real * second[:, 1] - grad_imag * second[:, 0],
        ],
        axis=1,
    ).reshape(-1, count)
    to_second = jnp.stack(
        [
            grad_real * first[:, 0] - grad_imag * first[:, 1],
            grad_real * first[:, 1] + grad_imag * first[:, 0],
        ],
        axis=1,
    ).reshape(-1, count)
    return add_to_stations(accum, to_first, to_second, stations)


def body(spectra, band_weights, pair_stations, block_live, windows, observed):
    n_pair = lax.axis_size("pair")
    n_day = lax.axis_size("day")
    per_block, bands, lags = observed.shape
    half = lags // 2
    day_count = spectra.shape[0]
    freq_count = spectra.shape[2]
    station_count = spectra.shape[3]
    days = day_count * n_day
    ordered = (
        pair_stations.reshape(n_pair, n_day, per_block, 2).transpose(1, 0, 2, 3).reshape(-1, 2)
    )
    flat_spectra = spectra.reshape(-1, station_count)
    first_rows, second_rows = gather_rows(flat_spectra, ordered)
    local_stack = cross_stack(first_rows, second_rows, day_count, freq_count)
    total = lax.psum(local_stack, "day")
    day_share = lax.dynamic_slice_in_dim(
        total, lax.axis_index("day") * (n_pair * per_block), n_pair * per_block, 1
    )
    pair_stack = lax.all_to_all(day_share, "pair", split_axis=1, concat_axis=2, tiled=True)
    weights_full = jnp.concatenate([band_weights, band_weights], axis=1)
    flat_stack = jnp.concatenate([pair_stack[0], pair_stack[1]], axis=1)
    weighted = (
        (flat_stack[:, None, :] * weights_full[None])
        .astype(jnp.bfloat16)
        .reshape(per_block * bands, lags)
    )
    live = jnp.arange(per_block, dtype=jnp.int32) < block_live[0]
    row_live = jnp.repeat(live, bands)
    lower_lag = windows[:, :, 0].reshape(-1)
    upper_lag = windows[:, :, 1].reshape(-1)
    observed_rows = observed.reshape(per_block * bands, lags)
    width = min(256, lags)
    forward_scale = 2.0 / math.sqrt(lags * days)
    adjoint_scale = 1.0 / math.sqrt(lags)

    def lag_step(index, accum):
        start = index * width
        block_table = table_block(start, width, lags)
        corr = forward_scale * jnp.dot(weighted, block_table, preferred_element_type=jnp.float32)
        lag_index = start + jnp.arange(width, dtype=jnp.int32)
        inside = (
            row_live[:, None]
            & (lag_index[None, :] >= lower_lag[:, None])
            & (lag_index[None, :] < upper_lag[:, None])
        )
        target = lax.dynamic_slice_in_dim(observed_rows, start, width, 1).astype(jnp.float32)
        misfit = jnp.where(inside, corr - target, 0.0).astype(jnp.bfloat16)
        return accum + lax.dot_general(
            misfit, block_table, (((1,), (1,)), ((), ())), preferred_element_type=jnp.float32
        )

    adjoint_rows = lax.fori_loop(
        0, lags // width, lag_step, jnp.zeros((per_block * bands, lags), jnp.float32)
    )
    summed = jnp.sum(adjoint_rows.reshape(per_block, bands, lags) * weights_full[None], axis=1)
    adjoint_spec = adjoint_scale * summed
    adjoint_split = adjoint_spec.reshape(per_block, 2, half).transpose(1, 0, 2)
    spread = lax.all_to_all(adjoint_split, "pair", split_axis=2, concat_axis=1, tiled=True)
    start_total = jnp.zeros((flat_spectra.shape[0], station_count), jnp.float32)
    all_pairs = lax.all_gather(spread, "day", axis=1, tiled=True)
    flat_out = station_terms(start_total, first_rows, second_rows, all_pairs, ordered, day_count)
    return flat_out.reshape(spectra.shape)


def solution(mesh):
    in_specs = (
        P("day", None, "pair", None),
        P(),
        P(),
        P(("pair", "day")),
        P(("pair", "day"), None, None),
        P(("pair", "day"), None, None),
    )
    out_specs = P("day", None, "pair", None)
    return jax.shard_map(body, mesh=mesh, in_specs=in_specs, out_specs=out_specs, check_vma=False)
```

profile of v0, /device:TPU:1, one launch (start us, length us, event | category | flops | bytes accessed | tf_op | source)
XLA Modules:
  0.0 495.4 jit_solution(16453960934737975883)
XLA Ops:
  8.3 4.5 while.49
  16.7 188.6 %all-reduce.2.cloned.1.call-done = f32[2,1536,64]{1,2,0:T(8,128)} async-done(((f32[2,1536,64]{1,2,0:T(8,128)}), f32[2,1536,64]{1,2,0:T(8,128)}) %all-reduce.2.cloned.1.call-update) | async-done | bytes 786448 | tf_op jit(solution)/shard_map/psum | solution.py:126
  207.2 7.7 %all-to-all-start = ((f32[32,1,384]{2,1,0:T(1,128)}), f32[32,1,384]{2,1,0:T(1,128)S(1)}, u32[]{:S(2)}, u32[]{:S(2)}) async-start(f32[32,1,384]{2,1,0:T(1,128)} %reshape.72), calls=%async_computation | async-start | bytes 98304 | tf_op jit(solution)/shard_map/all_to_all | solution.py:130
  214.9 9.1 %all-to-all-done = f32[32,1,384]{2,1,0:T(1,128)S(1)} async-done(((f32[32,1,384]{2,1,0:T(1,128)}), f32[32,1,384]{2,1,0:T(1,128)S(1)}, u32[]{:S(2)}, u32[]{:S(2)}) %all-to-all-start) | async-done | bytes 49184 | tf_op jit(solution)/shard_map/all_to_all | solution.py:130
  225.7 176.8 %while.51 = (s32[]{:T(128)}, f32[24,4096]{1,0:T(8,128)S(1)}, s32[3,8,1]{1,0,2:T(4,128)}, s32[3,8,1]{1,0,2:T(4,128)}, bf16[24,4096]{1,0:T(8,128)(2,1)}, /*index=5...) while((s32[]{:T(128)}, f32[24,4096]{1,0:T(8,128)S(1)}, ...), condition=%wide.wide.region_6.7_spmd.clone, body=%wide.wide.region_5.6_spmd.clone.sunk | while | flops 118413576 | bytes 7291664 | solution.py:163
  225.8 8.6 %cosine_convert_fusion.3 = (bf16[2048,256]{1,0:T(8,128)(2,1)S(1)}, bf16[2048,256]{1,0:T(8,128)(2,1)S(1)}) fusion(s32[256]{0:T(256)S(1)} %iota_add_fusion.3), kind=kLoop, calls=%fused_computation.26.clone.clone.1 | loop fusion | flops 8912896 | bytes 2098176 | tf_op jit(solution)/shard_map/convert.1
  234.6 2.2 convolution_add_fusion.3
  236.8 8.6 %cosine_convert_fusion.3 = (bf16[2048,256]{1,0:T(8,128)(2,1)S(1)}, bf16[2048,256]{1,0:T(8,128)(2,1)S(1)}) fusion(s32[256]{0:T(256)S(1)} %iota_add_fusion.3), kind=kLoop, calls=%fused_computation.26.clone.clone.1 | loop fusion | flops 8912896 | bytes 2098176 | tf_op jit(solution)/shard_map/convert.1
  245.6 2.2 convolution_add_fusion.3
  247.9 8.6 %cosine_convert_fusion.3 = (bf16[2048,256]{1,0:T(8,128)(2,1)S(1)}, bf16[2048,256]{1,0:T(8,128)(2,1)S(1)}) fusion(s32[256]{0:T(256)S(1)} %iota_add_fusion.3), kind=kLoop, calls=%fused_computation.26.clone.clone.1 | loop fusion | flops 8912896 | bytes 2098176 | tf_op jit(solution)/shard_map/convert.1
  256.7 2.2 convolution_add_fusion.3
  258.9 8.6 %cosine_convert_fusion.3 = (bf16[2048,256]{1,0:T(8,128)(2,1)S(1)}, bf16[2048,256]{1,0:T(8,128)(2,1)S(1)}) fusion(s32[256]{0:T(256)S(1)} %iota_add_fusion.3), kind=kLoop, calls=%fused_computation.26.clone.clone.1 | loop fusion | flops 8912896 | bytes 2098176 | tf_op jit(solution)/shard_map/convert.1
  267.7 2.2 convolution_add_fusion.3
  270.0 8.6 %cosine_convert_fusion.3 = (bf16[2048,256]{1,0:T(8,128)(2,1)S(1)}, bf16[2048,256]{1,0:T(8,128)(2,1)S(1)}) fusion(s32[256]{0:T(256)S(1)} %iota_add_fusion.3), kind=kLoop, calls=%fused_computation.26.clone.clone.1 | loop fusion | flops 8912896 | bytes 2098176 | tf_op jit(solution)/shard_map/convert.1
  278.8 2.2 convolution_add_fusion.3
  281.0 8.6 %cosine_convert_fusion.3 = (bf16[2048,256]{1,0:T(8,128)(2,1)S(1)}, bf16[2048,256]{1,0:T(8,128)(2,1)S(1)}) fusion(s32[256]{0:T(256)S(1)} %iota_add_fusion.3), kind=kLoop, calls=%fused_computation.26.clone.clone.1 | loop fusion | flops 8912896 | bytes 2098176 | tf_op jit(solution)/shard_map/convert.1
  289.8 2.2 convolution_add_fusion.3
  292.1 8.6 %cosine_convert_fusion.3 = (bf16[2048,256]{1,0:T(8,128)(2,1)S(1)}, bf16[2048,256]{1,0:T(8,128)(2,1)S(1)}) fusion(s32[256]{0:T(256)S(1)} %iota_add_fusion.3), kind=kLoop, calls=%fused_computation.26.clone.clone.1 | loop fusion | flops 8912896 | bytes 2098176 | tf_op jit(solution)/shard_map/convert.1
  300.9 2.2 convolution_add_fusion.3
  303.1 8.6 %cosine_convert_fusion.3 = (bf16[2048,256]{1,0:T(8,128)(2,1)S(1)}, bf16[2048,256]{1,0:T(8,128)(2,1)S(1)}) fusion(s32[256]{0:T(256)S(1)} %iota_add_fusion.3), kind=kLoop, calls=%fused_computation.26.clone.clone.1 | loop fusion | flops 8912896 | bytes 2098176 | tf_op jit(solution)/shard_map/convert.1
  311.9 2.2 convolution_add_fusion.3
  314.2 8.6 %cosine_convert_fusion.3 = (bf16[2048,256]{1,0:T(8,128)(2,1)S(1)}, bf16[2048,256]{1,0:T(8,128)(2,1)S(1)}) fusion(s32[256]{0:T(256)S(1)} %iota_add_fusion.3), kind=kLoop, calls=%fused_computation.26.clone.clone.1 | loop fusion | flops 8912896 | bytes 2098176 | tf_op jit(solution)/shard_map/convert.1
  323.0 2.2 convolution_add_fusion.3
  325.2 8.6 %cosine_convert_fusion.3 = (bf16[2048,256]{1,0:T(8,128)(2,1)S(1)}, bf16[2048,256]{1,0:T(8,128)(2,1)S(1)}) fusion(s32[256]{0:T(256)S(1)} %iota_add_fusion.3), kind=kLoop, calls=%fused_computation.26.clone.clone.1 | loop fusion | flops 8912896 | bytes 2098176 | tf_op jit(solution)/shard_map/convert.1
  334.0 2.2 convolution_add_fusion.3
  336.3 8.6 %cosine_convert_fusion.3 = (bf16[2048,256]{1,0:T(8,128)(2,1)S(1)}, bf16[2048,256]{1,0:T(8,128)(2,1)S(1)}) fusion(s32[256]{0:T(256)S(1)} %iota_add_fusion.3), kind=kLoop, calls=%fused_computation.26.clone.clone.1 | loop fusion | flops 8912896 | bytes 2098176 | tf_op jit(solution)/shard_map/convert.1
  345.1 2.2 convolution_add_fusion.3
  347.3 8.6 %cosine_convert_fusion.3 = (bf16[2048,256]{1,0:T(8,128)(2,1)S(1)}, bf16[2048,256]{1,0:T(8,128)(2,1)S(1)}) fusion(s32[256]{0:T(256)S(1)} %iota_add_fusion.3), kind=kLoop, calls=%fused_computation.26.clone.clone.1 | loop fusion | flops 8912896 | bytes 2098176 | tf_op jit(solution)/shard_map/convert.1
  356.1 2.2 convolution_add_fusion.3
  358.4 8.6 %cosine_convert_fusion.3 = (bf16[2048,256]{1,0:T(8,128)(2,1)S(1)}, bf16[2048,256]{1,0:T(8,128)(2,1)S(1)}) fusion(s32[256]{0:T(256)S(1)} %iota_add_fusion.3), kind=kLoop, calls=%fused_computation.26.clone.clone.1 | loop fusion | flops 8912896 | bytes 2098176 | tf_op jit(solution)/shard_map/convert.1
  367.2 2.2 convolution_add_fusion.3
  369.4 8.6 %cosine_convert_fusion.3 = (bf16[2048,256]{1,0:T(8,128)(2,1)S(1)}, bf16[2048,256]{1,0:T(8,128)(2,1)S(1)}) fusion(s32[256]{0:T(256)S(1)} %iota_add_fusion.3), kind=kLoop, calls=%fused_computation.26.clone.clone.1 | loop fusion | flops 8912896 | bytes 2098176 | tf_op jit(solution)/shard_map/convert.1
  378.2 2.2 convolution_add_fusion.3
  380.5 8.6 %cosine_convert_fusion.3 = (bf16[2048,256]{1,0:T(8,128)(2,1)S(1)}, bf16[2048,256]{1,0:T(8,128)(2,1)S(1)}) fusion(s32[256]{0:T(256)S(1)} %iota_add_fusion.3), kind=kLoop, calls=%fused_computation.26.clone.clone.1 | loop fusion | flops 8912896 | bytes 2098176 | tf_op jit(solution)/shard_map/convert.1
  389.3 2.2 convolution_add_fusion.3
  391.5 8.6 %cosine_convert_fusion.3 = (bf16[2048,256]{1,0:T(8,128)(2,1)S(1)}, bf16[2048,256]{1,0:T(8,128)(2,1)S(1)}) fusion(s32[256]{0:T(256)S(1)} %iota_add_fusion.3), kind=kLoop, calls=%fused_computation.26.clone.clone.1 | loop fusion | flops 8912896 | bytes 2098176 | tf_op jit(solution)/shard_map/convert.1
  400.3 2.2 convolution_add_fusion.3
  403.9 3.6 reshape.74
  407.5 3.9 all-to-all-start.1
  411.4 9.1 %all-to-all-done.1 = f32[32,1,384]{2,1,0:T(1,128)S(1)} async-done(((f32[32,1,384]{2,1,0:T(1,128)}), f32[32,1,384]{2,1,0:T(1,128)S(1)}, u32[]{:S(2)}, u32[]{:S(2)}) %all-to-all-start.1) | async-done | bytes 49184 | tf_op jit(solution)/shard_map/all_to_all | solution.py:169
  421.2 3.1 reshape.75
  425.5 39.5 %all_gather.3 = f32[2,1536,64]{2,0,1:T(2,128)S(1)} all-gather(f32[2,96,64]{2,0,1:T(2,128)S(1)} %bitcast.109), channel_id=1, replica_groups=mesh['pair'=32,'day'=16] {'day'}, dimensions={1}, use_global_device_ids=true | all-gather | bytes 835584 | tf_op jit(solution)/shard_map/all_gather | solution.py:171
  464.9 2.2 fusion.66
  468.5 2.1 copy.69
  475.0 12.5 %while.50 = (s32[]{:T(128)}, f32[256,1024]{1,0:T(8,128)S(1)}, f32[256,1536]{1,0:T(8,128)}, f32[256,1536]{1,0:T(8,128)}, s32[1536,2]{0,1:T(2,128)S(1)}, /*index=5...) while((s32[]{:T(128)}, f32[256,1024]{1,0:T(8,128)S(1)}, f32[256,1536]{1,0:T(8,128)}, ...), condition=%wide.region_9.10_spmd.clone.clone, body=%wide.region_8.9_spmd.clone.clone.sunk | while | flops 3224109056 | bytes 7352501 | solution.py:83
  477.1 2.1 fusion.88
  481.2 2.1 fusion.88
  485.4 2.1 fusion.88
  (140 shorter events, 31.5 us)
Async XLA Ops:
  6.5 1.8 copy-start.8
  6.5 198.8 %all-reduce.2.cloned.1.call-start = ((), (), s32[]{:S(2)}) async-start(), calls=%async_computation.2 | async-start | bytes 1572864 | tf_op jit(solution)/shard_map/psum | solution.py:126
  13.2 1.1 copy-start
  13.2 1.6 copy-start.2
  14.8 1.0 copy-start.7
  14.8 1.8 copy-start.4
  15.8 209.9 %copy-start.5 = (s32[3,8,1]{1,0,2:T(4,128)}, s32[3,8,1]{1,0,2:T(4,128)S(1)}, u32[]{:S(2)}) copy-start(s32[3,8,1]{1,0,2:T(4,128)S(1)} %copy.75) | copy-start | bytes 292
  15.9 209.8 %copy-start.6 = (s32[3,8,1]{1,0,2:T(4,128)}, s32[3,8,1]{1,0,2:T(4,128)S(1)}, u32[]{:S(2)}) copy-start(s32[3,8,1]{1,0,2:T(4,128)S(1)} %copy.76) | copy-start | bytes 292
  207.2 16.8 %all-to-all-start = ((f32[32,1,384]{2,1,0:T(1,128)}), f32[32,1,384]{2,1,0:T(1,128)S(1)}, u32[]{:S(2)}, u32[]{:S(2)}) async-start(f32[32,1,384]{2,1,0:T(1,128)} %reshape.72), calls=%async_computation | async-start | bytes 98304 | tf_op jit(solution)/shard_map/all_to_all | solution.py:130
  407.5 13.0 %all-to-all-start.1 = ((f32[32,1,384]{2,1,0:T(1,128)}), f32[32,1,384]{2,1,0:T(1,128)S(1)}, u32[]{:S(2)}, u32[]{:S(2)}) async-start(f32[32,1,384]{2,1,0:T(1,128)} %reshape.74), calls=%async_computation.1 | async-start | bytes 98304 | tf_op jit(solution)/shard_map/all_to_all | solution.py:169
  464.9 5.7 %copy-start.1 = (f32[2,2,64,1536]{3,2,1,0:T(8,128)S(1)}, f32[2,2,64,1536]{3,2,1,0:T(8,128)}, u32[]{:S(2)}) copy-start(f32[2,2,64,1536]{3,2,1,0:T(8,128)} %copy-done) | copy-start | bytes 4718596
  464.9 5.7 %copy-start.3 = (f32[2,2,64,1536]{3,2,1,0:T(8,128)S(1)}, f32[2,2,64,1536]{3,2,1,0:T(8,128)}, u32[]{:S(2)}) copy-start(f32[2,2,64,1536]{3,2,1,0:T(8,128)} %copy-done.2) | copy-start | bytes 4718596
  473.3 1.7 copy-start.9
  487.6 1.0 copy-start.10
Sparse Core Ops, SparseCore 0:
  15.9 189.3 all-reduce.1
where the time goes:
time: 497 us; the launch traced here: 495 us
  waiting for transfers between devices  207 us (42%)
  other arithmetic  148 us (30%)
  matrix products  45 us (9%)
  blocking collectives  39.5 us (8%)
  local copies, waits for them, and re-layouts  29.9 us (6%)
  between operations  14.4 us (3%)
  starting transfers between devices  11.5 us (2%)
    psum x1, waiting for transfers between devices, body(): total = lax.psum(local_stack, 'day')  189 us
    another operation x16, other arithmetic  138 us
    all_gather x1, blocking collectives, body(): all_pairs = lax.all_gather(spread, 'day', axis=1, tiled=True)  39.5 us
    dot_general x16, matrix products, lag_step(): lax.dot_general(misfit, block_table, (((1,), (1,)), ((), ())), preferred_...  35.5 us
    unnamed x29, local copies, waits for them, and re-layouts  10.3 us
  transfers between devices with their start and end apart: 3, of which 3 were waited for; matrix products, arithmetic and copies ran while one was open for 0% of the time, Pallas kernels for 0%

commit v1 on v0

--- a/solution.py
+++ b/solution.py
@@ -3,6 +3,11 @@
 import jax.numpy as jnp
 from jax import lax
 from jax.sharding import PartitionSpec as P
+
+
+def gather_and_add(x, mesh_axis):
+    shards = lax.all_gather(x, mesh_axis)
+    return jnp.sum(shards, axis=0)
 
 
 def table_block(start, width, lags):
@@ -123,7 +128,7 @@
     flat_spectra = spectra.reshape(-1, station_count)
     first_rows, second_rows = gather_rows(flat_spectra, ordered)
     local_stack = cross_stack(first_rows, second_rows, day_count, freq_count)
-    total = lax.psum(local_stack, "day")
+    total = gather_and_add(local_stack, "day")
     day_share = lax.dynamic_slice_in_dim(
         total, lax.axis_index("day") * (n_pair * per_block), n_pair * per_block, 1
     )

time: 497 us -> 460 us (0.926)
  waiting for transfers between devices: 207 us -> 169 us
  blocking collectives: 39.5 us -> 33.4 us
  other arithmetic: 148 us -> 154 us
    psum x1 -> x0, waiting for transfers between devices: 189 us -> none  [body(): total = lax.psum(local_stack, 'day')]
    all_gather x0 -> x1, waiting for transfers between devices: none -> 151 us  [gather_and_add(): shards = lax.all_gather(x, mesh_axis)]
    all_gather x1, blocking collectives: 39.5 us -> 33.4 us  [body(): all_pairs = lax.all_gather(spread, 'day', axis=1, tiled=True)]
    reduce_sum x0 -> x1, other arithmetic: none -> 5.85 us  [gather_and_add(): return jnp.sum(shards, axis=0)]
where the time goes in v1:
time: 460 us; the launch traced here: 457 us
  waiting for transfers between devices  169 us (37%)
  other arithmetic  154 us (33%)
  matrix products  45 us (10%)
  blocking collectives  33.4 us (7%)
  local copies, waits for them, and re-layouts  29 us (6%)
  between operations  14.4 us (3%)
  starting transfers between devices  11.5 us (2%)
    all_gather x1, waiting for transfers between devices, gather_and_add(): shards = lax.all_gather(x, mesh_axis)  151 us
    another operation x16, other arithmetic  138 us
    dot_general x16, matrix products, lag_step(): lax.dot_general(misfit, block_table, (((1,), (1,)), ((), ())), preferred_...  35.5 us
    all_gather x1, blocking collectives, body(): all_pairs = lax.all_gather(spread, 'day', axis=1, tiled=True)  33.4 us
    unnamed x29, local copies, waits for them, and re-layouts  10.3 us
  transfers between devices with their start and end apart: 3, of which 3 were waited for; matrix products, arithmetic and copies ran while one was open for 0% of the time, Pallas kernels for 0%

profile of v1, /device:TPU:1, one launch (start us, length us, event | category | flops | bytes accessed | tf_op | source)
XLA Modules:
  0.0 457.0 jit_solution(7891196654021470663)
XLA Ops:
  8.3 4.5 while.49
  16.7 151.5 %all-gather.3.cloned.1.call-done = f32[32,1536,64]{1,2,0:T(8,128)} async-done(((f32[2,1536,64]{1,2,0:T(8,128)}), f32[32,1536,64]{1,2,0:T(8,128)}) %all-gather.3.cloned.1.call-update) | async-done | bytes 12582928 | tf_op jit(solution)/shard_map/all_gather | solution.py:9
  168.2 5.8 %reduce_sum.38 = f32[2,1536,64]{1,2,0:T(8,128)S(1)} reduce(f32[16,2,1536,64]{2,3,1,0:T(8,128)} %bitcast.97, f32[]{:T(128)} %constant.151.clone.1), dimensions={0}, to_apply=%region_4.0 | reduce | flops 2949120 | bytes 13369348 | tf_op jit(solution)/shard_map/reduce_sum | solution.py:10
  175.0 7.5 %all-to-all-start = ((f32[32,1,384]{2,1,0:T(1,128)}), f32[32,1,384]{2,1,0:T(1,128)S(1)}, u32[]{:S(2)}, u32[]{:S(2)}) async-start(f32[32,1,384]{2,1,0:T(1,128)} %reshape.73), calls=%async_computation | async-start | bytes 98304 | tf_op jit(solution)/shard_map/all_to_all | solution.py:135
  182.5 9.1 %all-to-all-done = f32[32,1,384]{2,1,0:T(1,128)S(1)} async-done(((f32[32,1,384]{2,1,0:T(1,128)}), f32[32,1,384]{2,1,0:T(1,128)S(1)}, u32[]{:S(2)}, u32[]{:S(2)}) %all-to-all-start) | async-done | bytes 49184 | tf_op jit(solution)/shard_map/all_to_all | solution.py:135
  193.5 176.8 %while.51 = (s32[]{:T(128)}, f32[24,4096]{1,0:T(8,128)S(1)}, s32[3,8,1]{1,0,2:T(4,128)}, s32[3,8,1]{1,0,2:T(4,128)}, bf16[24,4096]{1,0:T(8,128)(2,1)}, /*index=5...) while((s32[]{:T(128)}, f32[24,4096]{1,0:T(8,128)S(1)}, ...), condition=%wide.wide.region_6.7_spmd.clone, body=%wide.wide.region_5.6_spmd.clone.sunk | while | flops 118413576 | bytes 7291664 | solution.py:168
  193.5 8.6 %cosine_convert_fusion.3 = (bf16[2048,256]{1,0:T(8,128)(2,1)S(1)}, bf16[2048,256]{1,0:T(8,128)(2,1)S(1)}) fusion(s32[256]{0:T(256)S(1)} %iota_add_fusion.3), kind=kLoop, calls=%fused_computation.26.clone.clone.1 | loop fusion | flops 8912896 | bytes 2098176 | tf_op jit(solution)/shard_map/convert.1
  202.3 2.2 convolution_add_fusion.3
  204.5 8.6 %cosine_convert_fusion.3 = (bf16[2048,256]{1,0:T(8,128)(2,1)S(1)}, bf16[2048,256]{1,0:T(8,128)(2,1)S(1)}) fusion(s32[256]{0:T(256)S(1)} %iota_add_fusion.3), kind=kLoop, calls=%fused_computation.26.clone.clone.1 | loop fusion | flops 8912896 | bytes 2098176 | tf_op jit(solution)/shard_map/convert.1
  213.3 2.2 convolution_add_fusion.3
  215.6 8.6 %cosine_convert_fusion.3 = (bf16[2048,256]{1,0:T(8,128)(2,1)S(1)}, bf16[2048,256]{1,0:T(8,128)(2,1)S(1)}) fusion(s32[256]{0:T(256)S(1)} %iota_add_fusion.3), kind=kLoop, calls=%fused_computation.26.clone.clone.1 | loop fusion | flops 8912896 | bytes 2098176 | tf_op jit(solution)/shard_map/convert.1
  224.4 2.2 convolution_add_fusion.3
  226.6 8.6 %cosine_convert_fusion.3 = (bf16[2048,256]{1,0:T(8,128)(2,1)S(1)}, bf16[2048,256]{1,0:T(8,128)(2,1)S(1)}) fusion(s32[256]{0:T(256)S(1)} %iota_add_fusion.3), kind=kLoop, calls=%fused_computation.26.clone.clone.1 | loop fusion | flops 8912896 | bytes 2098176 | tf_op jit(solution)/shard_map/convert.1
  235.4 2.2 convolution_add_fusion.3
  237.7 8.6 %cosine_convert_fusion.3 = (bf16[2048,256]{1,0:T(8,128)(2,1)S(1)}, bf16[2048,256]{1,0:T(8,128)(2,1)S(1)}) fusion(s32[256]{0:T(256)S(1)} %iota_add_fusion.3), kind=kLoop, calls=%fused_computation.26.clone.clone.1 | loop fusion | flops 8912896 | bytes 2098176 | tf_op jit(solution)/shard_map/convert.1
  246.5 2.2 convolution_add_fusion.3
  248.7 8.6 %cosine_convert_fusion.3 = (bf16[2048,256]{1,0:T(8,128)(2,1)S(1)}, bf16[2048,256]{1,0:T(8,128)(2,1)S(1)}) fusion(s32[256]{0:T(256)S(1)} %iota_add_fusion.3), kind=kLoop, calls=%fused_computation.26.clone.clone.1 | loop fusion | flops 8912896 | bytes 2098176 | tf_op jit(solution)/shard_map/convert.1
  257.5 2.2 convolution_add_fusion.3
  259.8 8.6 %cosine_convert_fusion.3 = (bf16[2048,256]{1,0:T(8,128)(2,1)S(1)}, bf16[2048,256]{1,0:T(8,128)(2,1)S(1)}) fusion(s32[256]{0:T(256)S(1)} %iota_add_fusion.3), kind=kLoop, calls=%fused_computation.26.clone.clone.1 | loop fusion | flops 8912896 | bytes 2098176 | tf_op jit(solution)/shard_map/convert.1
  268.6 2.2 convolution_add_fusion.3
  270.8 8.6 %cosine_convert_fusion.3 = (bf16[2048,256]{1,0:T(8,128)(2,1)S(1)}, bf16[2048,256]{1,0:T(8,128)(2,1)S(1)}) fusion(s32[256]{0:T(256)S(1)} %iota_add_fusion.3), kind=kLoop, calls=%fused_computation.26.clone.clone.1 | loop fusion | flops 8912896 | bytes 2098176 | tf_op jit(solution)/shard_map/convert.1
  279.6 2.2 convolution_add_fusion.3
  281.9 8.6 %cosine_convert_fusion.3 = (bf16[2048,256]{1,0:T(8,128)(2,1)S(1)}, bf16[2048,256]{1,0:T(8,128)(2,1)S(1)}) fusion(s32[256]{0:T(256)S(1)} %iota_add_fusion.3), kind=kLoop, calls=%fused_computation.26.clone.clone.1 | loop fusion | flops 8912896 | bytes 2098176 | tf_op jit(solution)/shard_map/convert.1
  290.7 2.2 convolution_add_fusion.3
  292.9 8.6 %cosine_convert_fusion.3 = (bf16[2048,256]{1,0:T(8,128)(2,1)S(1)}, bf16[2048,256]{1,0:T(8,128)(2,1)S(1)}) fusion(s32[256]{0:T(256)S(1)} %iota_add_fusion.3), kind=kLoop, calls=%fused_computation.26.clone.clone.1 | loop fusion | flops 8912896 | bytes 2098176 | tf_op jit(solution)/shard_map/convert.1
  301.8 2.2 convolution_add_fusion.3
  304.0 8.6 %cosine_convert_fusion.3 = (bf16[2048,256]{1,0:T(8,128)(2,1)S(1)}, bf16[2048,256]{1,0:T(8,128)(2,1)S(1)}) fusion(s32[256]{0:T(256)S(1)} %iota_add_fusion.3), kind=kLoop, calls=%fused_computation.26.clone.clone.1 | loop fusion | flops 8912896 | bytes 2098176 | tf_op jit(solution)/shard_map/convert.1
  312.8 2.2 convolution_add_fusion.3
  315.0 8.6 %cosine_convert_fusion.3 = (bf16[2048,256]{1,0:T(8,128)(2,1)S(1)}, bf16[2048,256]{1,0:T(8,128)(2,1)S(1)}) fusion(s32[256]{0:T(256)S(1)} %iota_add_fusion.3), kind=kLoop, calls=%fused_computation.26.clone.clone.1 | loop fusion | flops 8912896 | bytes 2098176 | tf_op jit(solution)/shard_map/convert.1
  323.9 2.2 convolution_add_fusion.3
  326.1 8.6 %cosine_convert_fusion.3 = (bf16[2048,256]{1,0:T(8,128)(2,1)S(1)}, bf16[2048,256]{1,0:T(8,128)(2,1)S(1)}) fusion(s32[256]{0:T(256)S(1)} %iota_add_fusion.3), kind=kLoop, calls=%fused_computation.26.clone.clone.1 | loop fusion | flops 8912896 | bytes 2098176 | tf_op jit(solution)/shard_map/convert.1
  334.9 2.2 convolution_add_fusion.3
  337.1 8.6 %cosine_convert_fusion.3 = (bf16[2048,256]{1,0:T(8,128)(2,1)S(1)}, bf16[2048,256]{1,0:T(8,128)(2,1)S(1)}) fusion(s32[256]{0:T(256)S(1)} %iota_add_fusion.3), kind=kLoop, calls=%fused_computation.26.clone.clone.1 | loop fusion | flops 8912896 | bytes 2098176 | tf_op jit(solution)/shard_map/convert.1
  346.0 2.2 convolution_add_fusion.3
  348.2 8.6 %cosine_convert_fusion.3 = (bf16[2048,256]{1,0:T(8,128)(2,1)S(1)}, bf16[2048,256]{1,0:T(8,128)(2,1)S(1)}) fusion(s32[256]{0:T(256)S(1)} %iota_add_fusion.3), kind=kLoop, calls=%fused_computation.26.clone.clone.1 | loop fusion | flops 8912896 | bytes 2098176 | tf_op jit(solution)/shard_map/convert.1
  357.0 2.2 convolution_add_fusion.3
  359.2 8.6 %cosine_convert_fusion.3 = (bf16[2048,256]{1,0:T(8,128)(2,1)S(1)}, bf16[2048,256]{1,0:T(8,128)(2,1)S(1)}) fusion(s32[256]{0:T(256)S(1)} %iota_add_fusion.3), kind=kLoop, calls=%fused_computation.26.clone.clone.1 | loop fusion | flops 8912896 | bytes 2098176 | tf_op jit(solution)/shard_map/convert.1
  368.0 2.2 convolution_add_fusion.3
  371.6 3.6 reshape.75
  375.2 4.0 all-to-all-start.1
  379.3 8.9 %all-to-all-done.1 = f32[32,1,384]{2,1,0:T(1,128)S(1)} async-done(((f32[32,1,384]{2,1,0:T(1,128)}), f32[32,1,384]{2,1,0:T(1,128)S(1)}, u32[]{:S(2)}, u32[]{:S(2)}) %all-to-all-start.1) | async-done | bytes 49184 | tf_op jit(solution)/shard_map/all_to_all | solution.py:174
  389.0 3.1 reshape.76
  393.2 33.4 %all_gather.11 = f32[2,1536,64]{2,0,1:T(2,128)S(1)} all-gather(f32[2,96,64]{2,0,1:T(2,128)S(1)} %bitcast.111), channel_id=1, replica_groups=mesh['pair'=32,'day'=16] {'day'}, dimensions={1}, use_global_device_ids=true | all-gather | bytes 835584 | tf_op jit(solution)/shard_map/all_gather | solution.py:176
  426.6 2.1 fusion.66
  430.1 2.1 copy.80
  436.7 12.5 %while.50 = (s32[]{:T(128)}, f32[256,1024]{1,0:T(8,128)S(1)}, f32[256,1536]{1,0:T(8,128)}, f32[256,1536]{1,0:T(8,128)}, s32[1536,2]{0,1:T(2,128)S(1)}, /*index=5...) while((s32[]{:T(128)}, f32[256,1024]{1,0:T(8,128)S(1)}, f32[256,1536]{1,0:T(8,128)}, ...), condition=%wide.region_9.10_spmd.clone.clone, body=%wide.region_8.9_spmd.clone.clone.sunk | while | flops 3224109056 | bytes 7352501 | solution.py:88
  438.7 2.1 fusion.88
  447.1 2.1 fusion.88
  (141 shorter events, 32.9 us)
Async XLA Ops:
  6.5 1.8 copy-start.8
  6.5 161.6 %all-gather.3.cloned.1.call-start = ((), (), s32[]{:S(2)}) async-start(), calls=%async_computation.2 | async-start | bytes 13369344 | tf_op jit(solution)/shard_map/all_gather | solution.py:9
  13.2 1.2 copy-start
  13.2 1.7 copy-start.2
  14.8 1.0 copy-start.7
  14.8 1.8 copy-start.4
  15.8 158.2 %copy-start.5 = (s32[3,8,1]{1,0,2:T(4,128)}, s32[3,8,1]{1,0,2:T(4,128)S(1)}, u32[]{:S(2)}) copy-start(s32[3,8,1]{1,0,2:T(4,128)S(1)} %copy.86) | copy-start | bytes 292
  15.9 158.1 %copy-start.6 = (s32[3,8,1]{1,0,2:T(4,128)}, s32[3,8,1]{1,0,2:T(4,128)S(1)}, u32[]{:S(2)}) copy-start(s32[3,8,1]{1,0,2:T(4,128)S(1)} %copy.87) | copy-start | bytes 292
  175.0 16.6 %all-to-all-start = ((f32[32,1,384]{2,1,0:T(1,128)}), f32[32,1,384]{2,1,0:T(1,128)S(1)}, u32[]{:S(2)}, u32[]{:S(2)}) async-start(f32[32,1,384]{2,1,0:T(1,128)} %reshape.73), calls=%async_computation | async-start | bytes 98304 | tf_op jit(solution)/shard_map/all_to_all | solution.py:135
  375.2 12.9 %all-to-all-start.1 = ((f32[32,1,384]{2,1,0:T(1,128)}), f32[32,1,384]{2,1,0:T(1,128)S(1)}, u32[]{:S(2)}, u32[]{:S(2)}) async-start(f32[32,1,384]{2,1,0:T(1,128)} %reshape.75), calls=%async_computation.1 | async-start | bytes 98304 | tf_op jit(solution)/shard_map/all_to_all | solution.py:174
  426.6 5.7 %copy-start.1 = (f32[2,2,64,1536]{3,2,1,0:T(8,128)S(1)}, f32[2,2,64,1536]{3,2,1,0:T(8,128)}, u32[]{:S(2)}) copy-start(f32[2,2,64,1536]{3,2,1,0:T(8,128)} %copy-done) | copy-start | bytes 4718596
  426.6 5.7 %copy-start.3 = (f32[2,2,64,1536]{3,2,1,0:T(8,128)S(1)}, f32[2,2,64,1536]{3,2,1,0:T(8,128)}, u32[]{:S(2)}) copy-start(f32[2,2,64,1536]{3,2,1,0:T(8,128)} %copy-done.2) | copy-start | bytes 4718596
  435.0 1.7 copy-start.9
  449.2 1.0 copy-start.10
Sparse Core Ops, SparseCore 0:
  15.9 152.2 all-gather.2
